TPU v7x, 512 devices: a whole 4x8x8 slice. The times are simulated.
512 devices in a mesh: frm: 32 (over y, z_lo), hgt: 4 (over x), wid: 4 (over z_hi, core).
Axes of the slice: x: 4, y: 8, z: 8 (z_hi: 2, z_lo: 4; z = z_hi * 4 + z_lo), core: 2. Of those that a mesh axis runs over, the one named last changes fastest.
Arguments:
- video: bfloat16 [1280, 1536, 512], P('frm', 'hgt', 'wid'), may hold values from -30 to 30
- height_factor: bfloat16 [1536, 256], P('hgt'), may hold values from -0.15625 to 0.15625
- width_factor: bfloat16 [512, 256], P('wid'), may hold values from -0.25 to 0.25
- start_basis: float32 [1280, 64], P('frm'), may hold values from -6 to 6
Outputs:
- gram: float32 [1280, 1280], P('frm', ('hgt', 'wid'))
- frame_factor: float32 [1280, 64], P('frm')
All inputs are finite; a program needn't handle non-finite values.
Results may differ from a plain program's by a relative error of at most 0.02.
Values may be sent and summed in bfloat16 or wider, within the bound.
No kernel may reach another device: no remote copies, remote signals or barrier semaphores. Data moves between devices by JAX's collectives and lax.ppermute only.
A program may use at most 64 MiB of HBM per device.

v0:
```python
import math

import jax
import jax.numpy as jnp
from jax import lax
from jax.sharding import PartitionSpec as P

ITERS = 3


def subspace(basis, apply_gram, steps):
    for step in range(steps):
        full_basis = lax.all_gather(basis, "frm", axis=0, tiled=True)
        product = apply_gram(full_basis)
        local_small = jnp.dot(product.T, product, precision=lax.Precision.HIGHEST)
        small = lax.psum(local_small, "frm")
        lower = jnp.linalg.cholesky(small)
        basis = lax.linalg.triangular_solve(
            lower, product, left_side=False, lower=True, transpose_a=True
        )
    return basis


def local(video, height_factor, width_factor, start_basis):
    rank_h = height_factor.shape[1]
    rank_w = width_factor.shape[1]
    frames_dev = video.shape[0]
    mid = lax.psum_scatter(
        jnp.einsum("fhw,hr->rfw", video, height_factor, preferred_element_type=jnp.float32).astype(
            jnp.bfloat16
        ),
        "hgt",
        scatter_dimension=0,
        tiled=True,
    )
    term = jnp.einsum("afw,wb->fab", mid, width_factor, preferred_element_type=jnp.float32)
    core = lax.psum_scatter(term.astype(jnp.bfloat16), "wid", scatter_dimension=2, tiled=True)
    core = core.reshape(frames_dev, -1)
    frm_count = lax.axis_size("frm")
    total_frames = frames_dev * frm_count
    partial_rows = lax.dot_general(
        core,
        lax.all_gather(core, "frm", axis=0, tiled=True),
        (((1,), (1,)), ((), ())),
        preferred_element_type=jnp.float32,
    )
    groups = lax.axis_size("hgt") * lax.axis_size("wid")
    block = total_frames // groups
    group = lax.axis_index("hgt") * lax.axis_size("wid") + lax.axis_index("wid")
    divisor = float(rank_h * rank_w)
    gram_rows = lax.psum(partial_rows, ("hgt", "wid")) / divisor
    gram_out = lax.dynamic_slice_in_dim(gram_rows, group * block, block, 1)

    def apply_gram(full_basis):
        return jnp.dot(gram_rows, full_basis, precision=lax.Precision.HIGHEST)

    basis = subspace(start_basis, apply_gram, ITERS)
    return (gram_out, basis * math.sqrt(total_frames))


def solution(mesh):
    return jax.shard_map(
        local,
        mesh=mesh,
        in_specs=(P("frm", "hgt", "wid"), P("hgt", None), P("wid", None), P("frm", None)),
        out_specs=(P("frm", ("hgt", "wid")), P("frm", None)),
        check_vma=False,
    )
```

profile of v0, /device:TPU:32, one launch (start us, length us, event | category | flops | bytes accessed | tf_op | source)
XLA Modules:
  0.0 1201.8 jit_solution(4732120565991118299)
XLA Ops:
  7.2 0.9 copy-done
  8.1 5.2 convolution_convert_fusion
  13.3 43.7 %reduce-scatter.5.cloned.1.call-done = bf16[64,40,128]{2,0,1:T(8,128)(2,1)} async-done(((bf16[256,40,128]{2,0,1:T(8,128)(2,1)}), bf16[64,40,128]{2,0,1:T(8,128)(2,1)}) %reduce-scatter.5.cloned.1.call-update) | async-done | bytes 655376 | tf_op jit(solution)/shard_map/reduce_scatter | solution.py:28
  57.0 1.8 fusion
  58.8 6.6 copy.33
  65.4 7.5 reshape.31
  73.0 54.3 %reduce-scatter.7.cloned.1.call-done = bf16[64,2560]{1,0:T(8,128)(2,1)} async-done(((bf16[256,2560]{1,0:T(8,128)(2,1)}), bf16[64,2560]{1,0:T(8,128)(2,1)}) %reduce-scatter.7.cloned.1.call-update) | async-done | bytes 327696
  127.3 2.9 reshape.32
  130.2 1.8 copy.21
  131.9 1.3 reshape.18
  133.3 231.7 %all-gather.2.cloned.1.call-done = bf16[1280,4096]{1,0:T(8,128)(2,1)} async-done(((bf16[40,4096]{1,0:T(8,128)(2,1)}), bf16[1280,4096]{1,0:T(8,128)(2,1)}) %all-gather.2.cloned.1.call-update) | async-done | bytes 10485776 | tf_op jit(solution)/shard_map/all_gather | solution.py:43
  365.0 8.0 fusion.21
  373.1 81.0 %all_gather.13 = f32[1280,64]{1,0:T(8,128)S(1)} all-gather(f32[40,64]{1,0:T(8,128)S(1)} %copy-done.3), channel_id=1, replica_groups=mesh['frm'=32,'hgt'=4,'wid'=4] {'frm'}, dimensions={0}, use_global_device_ids=true | all-gather | bytes 337920 | tf_op jit(solution)/shard_map/all_gather | solution.py:13
  454.1 97.3 %all-reduce.2.cloned.1.call-done = f32[40,1280]{1,0:T(8,128)} async-done(((f32[40,1280]{1,0:T(8,128)}), f32[40,1280]{1,0:T(8,128)}) %all-reduce.2.cloned.1.call-update) | async-done | bytes 204816 | tf_op jit(solution)/shard_map/psum | solution.py:51
  551.4 1.5 fusion.20
  553.1 150.1 %psum.29 = f32[64,64]{0,1:T(8,128)S(1)} all-reduce(f32[64,64]{0,1:T(8,128)S(1)} %fusion.22), channel_id=1, replica_groups=mesh['frm'=32,'hgt'=4,'wid'=4] {'frm'}, use_global_device_ids=true, to_apply=%region_3.0 | all-reduce | flops 4096 | bytes 32768 | tf_op jit(solution)/shard_map/psum | solution.py:16
  703.3 5.8 cholesky.59
  709.9 0.7 fusion.5
  710.5 4.9 custom-call.7
  715.6 76.4 %all_gather.14 = f32[1280,64]{1,0:T(8,128)S(1)} all-gather(f32[40,64]{1,0:T(8,128)S(1)} %convolution_bitcast_fusion.2), channel_id=1, replica_groups=mesh['frm'=32,'hgt'=4,'wid'=4] {'frm'}, dimensions={0}, use_global_device_ids=true | all-gather | bytes 337920 | tf_op jit(solution)/shard_map/all_gather | solution.py:13
  792.0 1.4 fusion.19
  793.7 149.5 %psum.30 = f32[64,64]{0,1:T(8,128)S(1)} all-reduce(f32[64,64]{0,1:T(8,128)S(1)} %fusion.23), channel_id=1, replica_groups=mesh['frm'=32,'hgt'=4,'wid'=4] {'frm'}, use_global_device_ids=true, to_apply=%region_6.9 | all-reduce | flops 4096 | bytes 32768 | tf_op jit(solution)/shard_map/psum | solution.py:16
  943.2 5.8 cholesky.70
  949.7 0.7 fusion.6
  950.4 4.9 custom-call.8
  955.5 76.3 %all_gather.15 = f32[1280,64]{1,0:T(8,128)S(1)} all-gather(f32[40,64]{1,0:T(8,128)S(1)} %convolution_bitcast_fusion.1), channel_id=1, replica_groups=mesh['frm'=32,'hgt'=4,'wid'=4] {'frm'}, dimensions={0}, use_global_device_ids=true | all-gather | bytes 337920 | tf_op jit(solution)/shard_map/all_gather | solution.py:13
  1032.5 149.1 %psum.31 = f32[64,64]{0,1:T(8,128)S(1)} all-reduce(f32[64,64]{0,1:T(8,128)S(1)} %fusion.24), channel_id=1, replica_groups=mesh['frm'=32,'hgt'=4,'wid'=4] {'frm'}, use_global_device_ids=true, to_apply=%region_7.10 | all-reduce | flops 4096 | bytes 32768 | tf_op jit(solution)/shard_map/psum | solution.py:16
  1181.7 5.8 cholesky.81
  1188.2 0.7 fusion.7
  1188.9 4.9 custom-call.9
  1193.8 0.8 fusion.1
  1194.6 0.7 constant_dynamic-slice_fusion
  (34 shorter events, 4.1 us)
Async XLA Ops:
  7.2 0.9 copy-start
  7.2 49.8 %copy-start.2 = (bf16[128,256]{1,0:T(8,128)(2,1)S(1)}, bf16[128,256]{1,0:T(8,128)(2,1)}, u32[]{:S(2)}) copy-start(bf16[128,256]{1,0:T(8,128)(2,1)} %param.9) | copy-start | bytes 196612
  7.2 49.8 %reduce-scatter.5.cloned.1.call-start = ((), (), s32[]{:S(2)}) async-start(), calls=%async_computation.2 | async-start | bytes 3276800 | tf_op jit(solution)/shard_map/reduce_scatter | solution.py:28
  13.3 114.0 %reduce-scatter.7.cloned.1.call-start = ((), (), s32[]{:S(2)}) async-start(), calls=%async_computation.5 | async-start | bytes 1638400
  72.9 292.1 %all-gather.2.cloned.1.call-start = ((), (), s32[]{:S(2)}) async-start(), calls=%async_computation.3 | async-start | bytes 10813440 | tf_op jit(solution)/shard_map/all_gather | solution.py:43
  133.2 239.9 %copy-start.3 = (f32[40,64]{1,0:T(8,128)S(1)}, f32[40,64]{1,0:T(8,128)}, u32[]{:S(2)}) copy-start(f32[40,64]{1,0:T(8,128)} %param.10) | copy-start | bytes 30724
  133.2 418.2 %all-reduce.2.cloned.1.call-start = ((), (), s32[]{:S(2)}) async-start(), calls=%async_computation.4 | async-start | bytes 409600 | tf_op jit(solution)/shard_map/psum | solution.py:51
  551.4 480.4 %copy-start.1 = (f32[40,1280]{1,0:T(8,128)S(1)}, f32[40,1280]{1,0:T(8,128)}, u32[]{:S(2)}) copy-start(f32[40,1280]{1,0:T(8,128)} %all-reduce.2.cloned.1.call-done) | copy-start | bytes 614404
Sparse Core Ops, SparseCore 0:
  13.4 43.5 reduce-scatter.4
  73.1 54.1 reduce-scatter.6
  133.3 231.6 all-gather.1
  373.2 178.1 all-reduce.1
where the time goes:
time: 1200 us
  blocking collectives  682 us (57%)
  waiting for transfers between devices  427 us (36%)
  other arithmetic  36.2 us (3%)
  local copies, waits for them, and re-layouts  21.8 us (2%)
  matrix products  20.2 us (2%)
  between operations  14 us (1%)
    psum x3, blocking collectives, subspace(): small = lax.psum(local_small, 'frm')  449 us
    all_gather x3, blocking collectives, subspace(): full_basis = lax.all_gather(basis, 'frm', axis=0, tiled=True)  234 us
    all_gather x1, waiting for transfers between devices, local(): lax.all_gather(core, 'frm', axis=0, tiled=True)  232 us
    psum x1, waiting for transfers between devices, local(): gram_rows = lax.psum(partial_rows, ('hgt', 'wid')) / divisor  97.3 us
    unnamed x5, waiting for transfers between devices  54.3 us
    reduce_scatter x1, waiting for transfers between devices, local(): lax.psum_scatter(jnp.einsum('fhw,hr->rfw', video, height_factor, preferre...  43.7 us
  transfers between devices with their start and end apart: 4, of which 4 were waited for; matrix products, arithmetic and copies ran while one was open for 0% of the time, Pallas kernels for 0%

commit v1 on v0

v1 whole, which is shorter than its diff:
```python
import math

import jax
import jax.numpy as jnp
from jax import lax
from jax.experimental import pallas as pl
from jax.experimental.pallas import tpu as pltpu
from jax.sharding import Mesh, PartitionSpec as P

ITERS = 3
Z_HI = 2
CORES = 2
Z_LO = 4
ALL = ("y", "zl", "x", "zh", "c")


def mid_kernel(video_ref, factor_ref, out_ref, acc):
    frames, _, _ = video_ref.shape
    rank = factor_ref.shape[0]

    @pl.loop(0, frames)
    def _(f):
        acc[pl.ds(pl.multiple_of(f * rank, rank), rank), :] = jnp.dot(
            factor_ref[...], video_ref[f], preferred_element_type=jnp.float32
        )

    @pl.loop(0, rank)
    def _(r):
        out_ref[r] = acc[pl.ds(r, frames, stride=rank), :].astype(out_ref.dtype)


def mid_partial(video, factor_t):
    frames, rows, cols = video.shape
    rank = factor_t.shape[0]
    return pl.pallas_call(
        mid_kernel,
        out_shape=jax.ShapeDtypeStruct((rank, frames, cols), jnp.bfloat16),
        in_specs=[pl.BlockSpec(memory_space=pltpu.VMEM)] * 2,
        out_specs=pl.BlockSpec(memory_space=pltpu.VMEM),
        scratch_shapes=[pltpu.VMEM((frames * rank, cols), jnp.float32)],
        compiler_params=pltpu.CompilerParams(vmem_limit_bytes=40 << 20),
        cost_estimate=pl.CostEstimate(
            flops=2 * frames * rows * cols * rank,
            bytes_accessed=2 * (frames * cols * (rows + rank) + rank * rows),
            transcendentals=0,
        ),
        name="mid_partial",
    )(video, factor_t)


def local(video, height_factor, width_factor, start_basis):
    rank_h = height_factor.shape[1]
    rank_w = width_factor.shape[1]
    frames_dev, _, cols = video.shape
    frm = lax.axis_index(("y", "zl"))
    core_at = lax.axis_index("c")
    total = frames_dev * lax.axis_size(("y", "zl"))

    width_pair = lax.all_gather(width_factor, "zh", axis=0)
    mid = mid_partial(video, height_factor.T)
    mid = lax.psum_scatter(mid, "x", scatter_dimension=0, tiled=True)

    mid = lax.all_to_all(mid, ("zh", "y", "zl"), 0, 0, tiled=True)
    mid = mid.reshape(Z_HI, total, cols)
    part = jnp.einsum("kfw,kws->fs", mid, width_pair, preferred_element_type=jnp.float32)
    half = rank_w // CORES
    low, high = part[:, :half], part[:, half:]
    first = core_at == 0
    sent = jnp.where(first, high, low).astype(jnp.bfloat16)
    came = lax.ppermute(sent, "c", [(0, 1), (1, 0)])
    kept = jnp.where(first, low, high).astype(jnp.bfloat16)
    core = (kept.astype(jnp.float32) + came.astype(jnp.float32)).astype(jnp.bfloat16)

    gram = lax.dot_general(core, core, (((1,), (1,)), ((), ())), preferred_element_type=jnp.float32)
    gram = gram / float(rank_h * rank_w)

    place = (lax.axis_index("x") == 0) & (lax.axis_index("zh") == 0) & first
    shard = jnp.where(place, start_basis, 0.0).T
    basis_t = lax.dynamic_update_slice(
        jnp.zeros((shard.shape[0], total), jnp.float32), shard, (0, frm * frames_dev)
    )
    both = lax.psum(jnp.concatenate([gram, basis_t], axis=0), ALL)
    gram, basis = both[:total], both[total:].T

    group = lax.axis_index(("x", "zh", "c"))
    block = total // lax.axis_size(("x", "zh", "c"))
    gram_out = lax.dynamic_slice(gram, (frm * frames_dev, group * block), (frames_dev, block))

    for _ in range(ITERS):
        product = jnp.dot(gram, basis, precision=lax.Precision.HIGHEST)
        small = jnp.dot(product.T, product, precision=lax.Precision.HIGHEST)
        lower = jnp.linalg.cholesky(small)
        basis = lax.linalg.triangular_solve(
            lower, product, left_side=False, lower=True, transpose_a=True
        )
    mine = lax.dynamic_slice_in_dim(basis, frm * frames_dev, frames_dev, 0)
    return (gram_out, mine * math.sqrt(total))


def solution(mesh):
    frm, hgt, _ = mesh.devices.shape
    fine = Mesh(
        mesh.devices.reshape(frm // Z_LO, Z_LO, hgt, Z_HI, CORES), ("y", "zl", "x", "zh", "c")
    )
    frm, hgt, wid = ("y", "zl"), "x", ("zh", "c")
    return jax.shard_map(
        local,
        mesh=fine,
        in_specs=(P(frm, hgt, wid), P(hgt, None), P(wid, None), P(frm, None)),
        out_specs=(P(frm, ("x", "zh", "c")), P(frm, None)),
        check_vma=False,
    )
```

time: 1200 us -> 483 us (0.40)
  the two profiles are of different devices: /device:TPU:32 before, /device:TPU:1 now
where the time goes in v1:
time: 483 us; the launch traced here: 481 us
  waiting for transfers between devices  332 us (69%)
  other arithmetic  39.7 us (8%)
  matrix products  31.8 us (7%)
  blocking collectives  21.1 us (4%)
  starting transfers between devices  17.6 us (4%)
  Pallas kernels  16.6 us (3%)
  between operations  14.3 us (3%)
  local copies, waits for them, and re-layouts  8.21 us (2%)
    psum x1, waiting for transfers between devices, local(): both = lax.psum(jnp.concatenate([gram, basis_t], axis=0), ALL)  287 us
    reduce_scatter x1, waiting for transfers between devices, local(): mid = lax.psum_scatter(mid, 'x', scatter_dimension=0, tiled=True)  45 us
    dot_general x3, matrix products, local(): product = jnp.dot(gram, basis, precision=lax.Precision.HIGHEST)  27.7 us
    all_gather x1, blocking collectives, local(): width_pair = lax.all_gather(width_factor, 'zh', axis=0)  21.1 us
    another operation x9, other arithmetic, local(): lower = jnp.linalg.cholesky(small)  19.6 us
    another operation x6, other arithmetic, local(): lax.linalg.triangular_solve(lower, product, left_side=False, lower=True,...  16.6 us
    pallas_call x1, Pallas kernels, mid_partial(): pl.pallas_call(mid_kernel, out_shape=jax.ShapeDtypeStruct((rank, frames,...  16.6 us
    all_to_all x1, starting transfers between devices, local(): mid = lax.all_to_all(mid, ('zh', 'y', 'zl'), 0, 0, tiled=True)  13 us
  transfers between devices with their start and end apart: 4, of which 3 were waited for; matrix products, arithmetic and copies ran while one was open for 0% of the time, Pallas kernels for 0%

profile of v1, /device:TPU:1, one launch (start us, length us, event | category | flops | bytes accessed | tf_op | source)
XLA Modules:
  0.0 481.5 jit_solution(1801926386393513750)
XLA Ops:
  7.2 1.1 copy.6
  8.3 2.1 copy-done
  10.4 16.6 %mid_partial.1 = bf16[256,40,128]{2,1,0:T(8,128)(2,1)} custom-call(bf16[40,384,128]{2,1,0:T(8,128)(2,1)S(1)} %copy-done, bf16[256,384]{1,0:T(8,128)(2,1)S(1)} %bitcast.53), custom_call_target="tpu_custom_call" | custom-call | flops 1006632960 | bytes 6750208 | tf_op jit(solution)/shard_map/mid_partial/pallas_call | solution.py:35
  27.1 45.0 %reduce-scatter.2.cloned.1.call-done = bf16[64,40,128]{2,1,0:T(8,128)(2,1)} async-done(((bf16[256,40,128]{2,1,0:T(8,128)(2,1)}), bf16[64,40,128]{2,1,0:T(8,128)(2,1)}) %reduce-scatter.2.cloned.1.call-update) | async-done | bytes 655376 | tf_op jit(solution)/shard_map/reduce_scatter | solution.py:61
  72.1 13.0 %all-to-all-start = ((bf16[64,40,128]{2,1,0:T(8,128)(2,1)}), bf16[64,40,128]{2,1,0:T(8,128)(2,1)S(1)}, u32[]{:S(2)}, u32[]{:S(2)}) async-start(bf16[64,40,128]{2,1,0:T(8,128)(2,1)} %reduce-scatter.2.cloned.1.call-done), calls=%async_computation.1 | async-start | bytes 1310720 | tf_op jit(solution)/shard_map/all_to_all | solution.py:63
  85.1 21.1 %all-gather = bf16[256,256]{1,0:T(8,128)(2,1)S(1)} all-gather(bf16[128,256]{1,0:T(8,128)(2,1)S(1)} %copy-done.1), channel_id=2, replica_groups=mesh['y'=8,'zl'=4,'x'=4,'zh'=2,'c'=2] {'zh'}, dimensions={0}, use_global_device_ids=true | all-gather | bytes 196608 | tf_op jit(solution)/shard_map/all_gather | solution.py:59
  106.6 4.5 collective-permute-start
  111.7 0.6 collective-permute-done
  112.3 1.0 convolution_multiply_fusion
  113.4 3.3 pad_maximum_fusion
  116.7 286.6 %all-reduce.2.cloned.1.call-done = f32[1344,1280]{1,0:T(8,128)} async-done(((f32[1344,1280]{1,0:T(8,128)}), f32[1344,1280]{1,0:T(8,128)}) %all-reduce.2.cloned.1.call-update) | async-done | bytes 6881296 | tf_op jit(solution)/shard_map/psum | solution.py:82
  403.3 9.2 %fusion = f32[1280,64]{0,1:T(8,128)S(1)} fusion(f32[1344,1280]{1,0:T(8,128)} %all-reduce.2.cloned.1.call-done), kind=kOutput, calls=%fused_computation.9 | convolution fusion | flops 1258291200 | bytes 7208960 | tf_op jit(solution)/shard_map/dot_general | solution.py:90
  413.0 5.8 %cholesky.59 = f32[64,64]{1,0:T(8,128)S(1)} custom-call(f32[64,64]{1,0:T(8,128)S(1)} %fusion.11), custom_call_target="Cholesky" | custom-call | tf_op jit(solution)/shard_map/jit(cholesky)/cholesky | solution.py:92
  418.9 0.6 compare_reduce_fusion.2
  419.5 0.7 fusion.3
  420.2 4.9 %custom-call.7 = f32[1,64,64]{1,2,0:T(8,128)S(1)} custom-call(f32[1,64,64]{2,1,0:T(8,128)S(1)} %fusion.3), custom_call_target="InvertDiagBlocksLowerTriangular" | custom-call | tf_op jit(solution)/shard_map/triangular_solve/custom-call.0 | solution.py:93
  425.1 0.5 convolution_bitcast_fusion.3
  425.6 9.4 %fusion.18 = f32[1280,64]{0,1:T(8,128)S(1)} fusion(f32[1280,64]{0,1:T(8,128)S(1)} %convolution_bitcast_fusion.3, f32[1344,1280]{1,0:T(8,128)} %all-reduce.2.cloned.1.call-done), kind=kOutput, calls=%fused_computation.41 | convolution fusion | flops 1258291200 | bytes 7208960 | tf_op jit(solution)/shard_map/dot_general | solution.py:90
  435.4 5.8 %cholesky.70 = f32[64,64]{1,0:T(8,128)S(1)} custom-call(f32[64,64]{1,0:T(8,128)S(1)} %fusion.9), custom_call_target="Cholesky" | custom-call | tf_op jit(solution)/shard_map/jit(cholesky)/cholesky | solution.py:92
  441.3 0.6 compare_reduce_fusion.1
  442.0 0.7 fusion.4
  442.6 4.9 %custom-call.8 = f32[1,64,64]{1,2,0:T(8,128)S(1)} custom-call(f32[1,64,64]{2,1,0:T(8,128)S(1)} %fusion.4), custom_call_target="InvertDiagBlocksLowerTriangular" | custom-call | tf_op jit(solution)/shard_map/triangular_solve/custom-call.0 | solution.py:93
  447.5 0.5 convolution_bitcast_fusion.2
  448.0 9.2 %fusion.16 = f32[1280,64]{0,1:T(8,128)S(1)} fusion(f32[1280,64]{0,1:T(8,128)S(1)} %convolution_bitcast_fusion.2, f32[1344,1280]{1,0:T(8,128)} %all-reduce.2.cloned.1.call-done), kind=kOutput, calls=%fused_computation.39 | convolution fusion | flops 1258291200 | bytes 7208960 | tf_op jit(solution)/shard_map/dot_general | solution.py:90
  457.7 5.8 %cholesky.81 = f32[64,64]{1,0:T(8,128)S(1)} custom-call(f32[64,64]{1,0:T(8,128)S(1)} %fusion.7), custom_call_target="Cholesky" | custom-call | tf_op jit(solution)/shard_map/jit(cholesky)/cholesky | solution.py:92
  463.6 0.6 compare_reduce_fusion
  464.3 0.7 fusion.5
  464.9 4.9 %custom-call.9 = f32[1,64,64]{1,2,0:T(8,128)S(1)} custom-call(f32[1,64,64]{2,1,0:T(8,128)S(1)} %fusion.5), custom_call_target="InvertDiagBlocksLowerTriangular" | custom-call | tf_op jit(solution)/shard_map/triangular_solve/custom-call.0 | solution.py:93
  469.8 0.5 convolution_bitcast_fusion.1
  470.4 0.7 copy.11
  471.1 2.9 slice-done
  473.9 0.7 dynamic_slice.6
  (30 shorter events, 2.7 us)
Async XLA Ops:
  7.2 77.9 %copy-start.1 = (bf16[128,256]{1,0:T(8,128)(2,1)S(1)}, bf16[128,256]{1,0:T(8,128)(2,1)}, u32[]{:S(2)}) copy-start(bf16[128,256]{1,0:T(8,128)(2,1)} %param.9) | copy-start | bytes 196612
  7.2 64.9 %reduce-scatter.2.cloned.1.call-start = ((), (), s32[]{:S(2)}) async-start(), calls=%async_computation.2 | async-start | bytes 3276800 | tf_op jit(solution)/shard_map/reduce_scatter | solution.py:61
  8.3 2.1 copy-start
  10.4 100.7 %copy-start.2 = (f32[40,64]{1,0:T(8,128)S(1)}, f32[40,64]{1,0:T(8,128)}, u32[]{:S(2)}) copy-start(f32[40,64]{1,0:T(8,128)} %param.10) | copy-start | bytes 30724
  72.1 34.1 %all-to-all-start = ((bf16[64,40,128]{2,1,0:T(8,128)(2,1)}), bf16[64,40,128]{2,1,0:T(8,128)(2,1)S(1)}, u32[]{:S(2)}, u32[]{:S(2)}) async-start(bf16[64,40,128]{2,1,0:T(8,128)(2,1)} %reduce-scatter.2.cloned.1.call-done), calls=%async_computation.1 | async-start | bytes 1310720 | tf_op jit(solution)/shard_map/all_to_all | solution.py:63
  85.0 318.2 %all-reduce.2.cloned.1.call-start = ((), (), s32[]{:S(2)}) async-start(), calls=%async_computation.3 | async-start | bytes 13762560 | tf_op jit(solution)/shard_map/psum | solution.py:82
  106.6 5.8 %collective-permute-start = (bf16[1280,128]{1,0:T(8,128)(2,1)S(1)}, bf16[1280,128]{1,0:T(8,128)(2,1)S(1)}, u32[]{:S(2)}, u32[]{:S(2)}) collective-permute-start(bf16[1280,128]{1,0:T(8,128)(2,1)S(1)} %select_convert_fusion), channel_id=1, source_target_pairs={{0,1},{1,0},{2,3},{3,2},{4,5},{5,4},{6,7},{7,6},{8,9},{9,8},{10,11... | collective-permute-start | bytes 983048 | tf_op jit(solution)/shard_map/ppermute | solution.py:70
  471.1 2.9 slice-start
Sparse Core Ops, SparseCore 0:
  27.2 44.8 reduce-scatter.1
  116.8 286.4 all-reduce.1
